TPU v7x, 256 devices: a whole 4x4x8 slice. The times are simulated.
256 devices in a mesh: rep: 32 (over z, y_lo, core), fsdp: 8 (over y_hi, x).
Axes of the slice: x: 4, y: 4 (y_hi: 2, y_lo: 2; y = y_hi * 2 + y_lo), z: 8, core: 2. Of those that a mesh axis runs over, the one named last changes fastest.
Arguments:
- tokens: bfloat16 [32768, 1536], P(('rep', 'fsdp')), may hold values from -6 to 6
- segment_ids: int32 [32768], P('rep'), may hold values from 0 to 3, as said below
- routes: int32 [32768, 6], P(('rep', 'fsdp')), may hold values from 0 to 7, all different within a row
- gain_attn: bfloat16 [1536], P('fsdp'), may hold values from 0.099609375 to 1.8984375
- w_query: bfloat16 [1536, 1536], P('fsdp'), may hold values from -0.3125 to 0.3125
- w_key: bfloat16 [1536, 512], P('fsdp'), may hold values from -0.15625 to 0.15625
- w_value: bfloat16 [1536, 512], P('fsdp'), may hold values from -0.15625 to 0.15625
- w_out: bfloat16 [1536, 1536], P('fsdp'), may hold values from -0.625 to 0.625
- gain_ffn: bfloat16 [1536], P('fsdp'), may hold values from 0.099609375 to 1.8984375
- w_router: bfloat16 [1536, 8], P('fsdp'), may hold values from -0.078125 to 0.078125
- w_shared_in: bfloat16 [1536, 2048], P('fsdp'), may hold values from -0.15625 to 0.15625
- w_shared_out: bfloat16 [1024, 1536], P('fsdp'), may hold values from -0.375 to 0.375
- w_expert_in: bfloat16 [1536, 8, 1024], P('fsdp'), may hold values from -0.15625 to 0.15625
- w_expert_out: bfloat16 [8, 512, 1536], P(None, 'fsdp'), may hold values from -1 to 1
- cotangent: bfloat16 [32768, 1536], P(('rep', 'fsdp')), may hold values from -6 to 6
Outputs:
- result: bfloat16 [32768, 1536], P(('rep', 'fsdp'))
- grad_input: bfloat16 [32768, 1536], P(('rep', 'fsdp'))
- grad_gain_attn: float32 [1536], P('fsdp')
- grad_query: float32 [1536, 1536], P('fsdp')
- grad_key: float32 [1536, 512], P('fsdp')
- grad_value: float32 [1536, 512], P('fsdp')
- grad_out: float32 [1536, 1536], P('fsdp')
- grad_gain_ffn: float32 [1536], P('fsdp')
- grad_router: float32 [1536, 8], P('fsdp')
- grad_shared_in: float32 [1536, 2048], P('fsdp')
- grad_shared_out: float32 [1024, 1536], P('fsdp')
- grad_expert_in: float32 [1536, 8, 1024], P('fsdp')
- grad_expert_out: float32 [8, 512, 1536], P(None, 'fsdp')
Inputs may be any that keep to these rules, and one draw needn't show every extreme that they name: `segment_ids`: within each sequence of 1024 tokens, documents 1, 2, 3 follow one another and padding 0 closes the sequence; document 2 begins on the sequence's first device and ends on its last. `routes`: 6 different experts for each token.
All inputs are finite; a program needn't handle non-finite values.
Results may differ from a plain program's by a relative error of at most 0.03.
Values may be sent and summed in bfloat16 or wider, within the bound.
No kernel may reach another device: no remote copies, remote signals or barrier semaphores. Data moves between devices by JAX's collectives and lax.ppermute only.
A program may use at most 256 MiB of HBM per device.

v0:
```python
import math
import jax
import jax.numpy as jnp
from jax import lax
from jax.sharding import PartitionSpec as P

HEADS = 12
KV_HEADS = 4
HEAD = 128
FE = 512
FS = 1024
eps_norm = 1e-05


def side_by_side(arrays, axis, dim, along):
    widths = [math.prod(a.shape[along:]) for a in arrays]
    both = jnp.concatenate(
        [a.reshape(*a.shape[:along], w) for a, w in zip(arrays, widths)], axis=along
    )
    whole = lax.all_gather(both, axis, axis=dim, tiled=True)
    pieces = jnp.split(whole, [sum(widths[:k]) for k in range(1, len(widths))], axis=along)
    return tuple(
        (b.reshape(*whole.shape[:along], *a.shape[along:]) for a, b in zip(arrays, pieces))
    )


def side_by_side_2(arrays, axis, dim, along):
    ends, at = ([], 0)
    for a in arrays[:-1]:
        at += a.shape[along]
        ends.append(at)
    both = jnp.concatenate(arrays, axis=along)
    return tuple(jnp.split(lax.all_gather(both, axis, axis=dim, tiled=True), ends, axis=along))


def joined_along(pieces, dim):
    lengths = list(pieces.shape[1:])
    lengths[dim] *= pieces.shape[0]
    return jnp.moveaxis(pieces, 0, dim).reshape(lengths)


def gather_packed(arrays, axis, dims):
    flat = jnp.concatenate([a.reshape(-1) for a in arrays])
    lines, at, gathered = (lax.all_gather(flat, axis), 0, [])
    for a, dim in zip(arrays, dims):
        pieces = lines[:, at : at + a.size].reshape(-1, *a.shape)
        gathered.append(joined_along(pieces, dim))
        at += a.size
    return tuple(gathered)


def in_blocks(array, dim, length):
    before, after = (array.shape[:dim], array.shape[dim + 1 :])
    return jnp.moveaxis(array.reshape(*before, length, -1, *after), dim, 0)


def summed_on_arrival(array, axis, dim):
    length = lax.axis_size(axis)
    pieces = lax.all_to_all(in_blocks(array, dim, length), axis, 0, 0, tiled=True)
    return jnp.sum(pieces, axis=0)


def in_one_piece(arrays, axis, dim, along):
    widths = [a.shape[along] for a in arrays]
    both = jnp.concatenate(arrays, axis=along)
    whole = lax.psum_scatter(both, axis, scatter_dimension=dim, tiled=True)
    return tuple(jnp.split(whole, [sum(widths[:k]) for k in range(1, len(widths))], axis=along))


def sent_together(arrays, axis, dim, along):
    columns = [a.reshape(*a.shape[:along], -1) for a in arrays]
    both = jnp.concatenate(columns, axis=along)
    whole, at, gathered = (lax.psum_scatter(both, axis, scatter_dimension=dim, tiled=True), 0, [])
    for a, column in zip(arrays, columns):
        section = whole[..., at : at + column.shape[along]]
        gathered.append(section.reshape(*section.shape[:along], *a.shape[along:]))
        at += column.shape[along]
    return tuple(gathered)


def dot_rows(left, right):
    return lax.dot_general(
        left, right, (((1,), (1,)), ((), ())), preferred_element_type=jnp.float32
    )


def dot_cols(left, right):
    return lax.dot_general(
        left, right, (((0,), (0,)), ((), ())), preferred_element_type=jnp.float32
    )


def normalize(values):
    factor = lax.rsqrt(jnp.mean(values * values, axis=-1, keepdims=True) + eps_norm)
    return (values * factor, factor)


def norm_back(grad_normed, unit, factor, gain):
    scaled = grad_normed * gain
    gain_grad = jnp.sum(grad_normed * unit, axis=0)
    inner = jnp.mean(scaled * unit, axis=-1, keepdims=True)
    return (factor * (scaled - unit * inner), gain_grad)


def silu_slope(values, sig):
    return sig * (1.0 + values * (1.0 - sig))


def shards(
    tokens,
    segment_ids,
    routes,
    gain_attn,
    w_query,
    w_key,
    w_value,
    w_out,
    gain_ffn,
    w_router,
    w_shared_in,
    w_shared_out,
    w_expert_in,
    w_expert_out,
    cotangent,
):
    local_rows = tokens.shape[0]
    group_len = segment_ids.shape[0]
    per_group = HEADS // KV_HEADS
    qk_scale = 1.0 / math.sqrt(HEAD)
    experts_count = w_router.shape[1]
    start_row = lax.axis_index("fsdp") * local_rows
    seg_local = lax.dynamic_slice_in_dim(segment_ids, start_row, local_rows)
    query_pos = start_row + jnp.arange(local_rows, dtype=jnp.int32)
    key_pos = jnp.arange(group_len, dtype=jnp.int32)
    allowed = (query_pos[:, None] == key_pos[None, :]) | (key_pos[None, :] < query_pos[:, None]) & (
        seg_local[:, None] == segment_ids[None, :]
    ) & (segment_ids[None, :] != 0)
    inputs = tokens.astype(jnp.float32)
    attn_in = side_by_side((gain_attn, w_query, w_key, w_value), "fsdp", 0, 1)
    unit_one, factor_one = normalize(inputs)
    gain_one = attn_in[0].astype(jnp.float32)
    normed_one = (unit_one * gain_one).astype(jnp.bfloat16)
    query = jnp.dot(normed_one, attn_in[1], preferred_element_type=jnp.float32).astype(jnp.bfloat16)
    key_local = jnp.dot(normed_one, attn_in[2], preferred_element_type=jnp.float32).astype(
        jnp.bfloat16
    )
    value_local = jnp.dot(normed_one, attn_in[3], preferred_element_type=jnp.float32).astype(
        jnp.bfloat16
    )
    keys_all, values_all = side_by_side_2((key_local, value_local), "fsdp", 0, 1)
    query_heads = query.reshape(local_rows, KV_HEADS, per_group, HEAD)
    key_heads = keys_all.reshape(group_len, KV_HEADS, HEAD)
    value_heads = values_all.reshape(group_len, KV_HEADS, HEAD)

    def scores_of():
        raw = (
            jnp.einsum("tkgd,skd->kgts", query_heads, key_heads, preferred_element_type=jnp.float32)
            * qk_scale
        )
        return jnp.where(allowed[None, None], raw, -1e30)

    scores = scores_of()
    top_score = jnp.max(scores, axis=-1, keepdims=True)
    expo = jnp.exp(scores - top_score)
    total = jnp.sum(expo, axis=-1, keepdims=True)
    log_total = top_score + jnp.log(total)
    probs = (expo / total).astype(jnp.bfloat16)
    attended = jnp.einsum("kgts,skd->tkgd", probs, value_heads, preferred_element_type=jnp.float32)
    attended = attended.reshape(local_rows, HEADS * HEAD).astype(jnp.bfloat16)
    out_full = lax.all_gather(w_out, "fsdp", axis=0, tiled=True)
    hidden = inputs + jnp.dot(attended, out_full, preferred_element_type=jnp.float32)
    ffn_in = (
        lax.all_gather(gain_ffn, "fsdp", axis=0, tiled=True),
        lax.all_gather(w_router, "fsdp", axis=0, tiled=True),
        lax.all_gather(w_shared_in, "fsdp", axis=0, tiled=True),
        lax.all_gather(w_expert_in, "fsdp", axis=0, tiled=True),
    )
    unit_two, factor_two = normalize(hidden)
    gain_two = ffn_in[0].astype(jnp.float32)
    normed_two = (unit_two * gain_two).astype(jnp.bfloat16)
    logits = jnp.dot(normed_two, ffn_in[1], preferred_element_type=jnp.float32)
    chosen = jnp.sum(
        (routes[:, :, None] == jnp.arange(experts_count, dtype=jnp.int32)[None, None, :]).astype(
            jnp.float32
        ),
        axis=1,
    )
    weighted = chosen * jnp.exp(logits)
    gates = weighted / jnp.sum(weighted, axis=-1, keepdims=True)
    expert_pre = jnp.einsum(
        "td,def->tef", normed_two, ffn_in[3], preferred_element_type=jnp.float32
    )
    gate_part = expert_pre[:, :, :FE]
    up_part = expert_pre[:, :, FE:]
    gate_sig = jax.nn.sigmoid(gate_part)
    activ = gate_part * gate_sig * up_part
    mixed = (gates[:, :, None] * activ).astype(jnp.bfloat16)
    shared_pre = jnp.dot(normed_two, ffn_in[2], preferred_element_type=jnp.float32)
    shared_gate = shared_pre[:, :FS]
    shared_up = shared_pre[:, FS:]
    shared_sig = jax.nn.sigmoid(shared_gate)
    shared_act = (shared_gate * shared_sig * shared_up).astype(jnp.bfloat16)
    ffn_out = gather_packed((w_expert_out, w_shared_out), "fsdp", (1, 0))
    result = hidden + jnp.einsum(
        "tef,efd->td", mixed, ffn_out[0], preferred_element_type=jnp.float32
    )
    result = result + jnp.dot(shared_act, ffn_out[1], preferred_element_type=jnp.float32)
    grad_top = cotangent.astype(jnp.float32)
    grad_mixed = jnp.einsum(
        "td,efd->tef", cotangent, ffn_out[0], preferred_element_type=jnp.float32
    )
    grad_shared = dot_rows(cotangent, ffn_out[1])
    grad_gates = jnp.sum(grad_mixed * activ, axis=-1)
    grad_activ = grad_mixed * gates[:, :, None]
    grad_pre = jnp.concatenate(
        [grad_activ * up_part * silu_slope(gate_part, gate_sig), grad_activ * gate_part * gate_sig],
        axis=-1,
    ).astype(jnp.bfloat16)
    grad_logits = (
        gates * (grad_gates - jnp.sum(gates * grad_gates, axis=-1, keepdims=True))
    ).astype(jnp.bfloat16)
    grad_spre = jnp.concatenate(
        [
            grad_shared * shared_up * silu_slope(shared_gate, shared_sig),
            grad_shared * shared_gate * shared_sig,
        ],
        axis=-1,
    ).astype(jnp.bfloat16)
    router_back, shared_back, expert_back = (ffn_in[1], ffn_in[2], ffn_in[3])
    grad_normed_two = jnp.einsum(
        "tef,def->td", grad_pre, expert_back, preferred_element_type=jnp.float32
    )
    grad_normed_two = (
        grad_normed_two + dot_rows(grad_spre, shared_back) + dot_rows(grad_logits, router_back)
    )
    grad_norm_two, grad_gain_ffn = norm_back(grad_normed_two, unit_two, factor_two, gain_two)
    grad_hidden = grad_top + grad_norm_two
    width_own = w_router.shape[0]
    col_start = lax.axis_index("fsdp") * width_own
    fe_own = w_expert_out.shape[1]
    fe_start = lax.axis_index("fsdp") * fe_own
    fs_own = w_shared_out.shape[0]
    fs_start = lax.axis_index("fsdp") * fs_own
    pieces = side_by_side((normed_two, grad_pre, grad_spre, grad_logits), "fsdp", 0, 1)
    part_normed = lax.dynamic_slice_in_dim(pieces[0], col_start, width_own, 1)
    router_part = dot_cols(part_normed, pieces[3])
    shared_part = dot_cols(part_normed, pieces[2])
    expert_part = jnp.einsum(
        "td,tef->def", part_normed, pieces[1], preferred_element_type=jnp.float32
    )
    shared_in_own = shared_part
    expert_in_own = expert_part
    pieces = side_by_side((mixed, shared_act, cotangent), "fsdp", 0, 1)
    part_mixed = lax.dynamic_slice_in_dim(pieces[0], fe_start, fe_own, 2)
    part_shared = lax.dynamic_slice_in_dim(pieces[1], fs_start, fs_own, 1)
    expert_part = jnp.einsum(
        "tef,td->efd", part_mixed, pieces[2], preferred_element_type=jnp.float32
    )
    shared_part = dot_cols(part_shared, pieces[2])
    gain_own = summed_on_arrival(grad_gain_ffn, "fsdp", 0)
    ffn_owned = (gain_own, router_part, shared_in_own, expert_in_own, shared_part, expert_part)
    hidden_low = grad_hidden.astype(jnp.bfloat16)
    grad_out = dot_cols(attended, hidden_low)
    grad_att = dot_rows(hidden_low, out_full).astype(jnp.bfloat16)
    grad_heads = grad_att.reshape(local_rows, KV_HEADS, per_group, HEAD)
    probs_again = jnp.exp(scores_of() - log_total)
    grad_probs = jnp.einsum(
        "tkgd,skd->kgts", grad_heads, value_heads, preferred_element_type=jnp.float32
    )
    inner = jnp.sum(probs_again * grad_probs, axis=-1, keepdims=True)
    grad_scores = (probs_again * (grad_probs - inner)).astype(jnp.bfloat16)
    grad_query_rows = (
        jnp.einsum("kgts,skd->tkgd", grad_scores, key_heads, preferred_element_type=jnp.float32)
        * qk_scale
    )
    grad_query_rows = grad_query_rows.reshape(local_rows, HEADS * HEAD).astype(jnp.bfloat16)
    grad_keys_all = (
        jnp.einsum("kgts,tkgd->skd", grad_scores, query_heads, preferred_element_type=jnp.float32)
        * qk_scale
    )
    grad_values_all = jnp.einsum(
        "kgts,tkgd->skd",
        probs_again.astype(jnp.bfloat16),
        grad_heads,
        preferred_element_type=jnp.float32,
    )
    key_sum, value_sum = tuple(
        (
            part.astype(jnp.float32)
            for part in in_one_piece(
                (
                    grad_keys_all.reshape(group_len, KV_HEADS * HEAD).astype(jnp.bfloat16),
                    grad_values_all.reshape(group_len, KV_HEADS * HEAD).astype(jnp.bfloat16),
                ),
                "fsdp",
                0,
                1,
            )
        )
    )
    grad_key_rows = key_sum.astype(jnp.bfloat16)
    grad_value_rows = value_sum.astype(jnp.bfloat16)
    query_back, key_back, value_back = (attn_in[1], attn_in[2], attn_in[3])
    grad_normed_one = (
        dot_rows(grad_query_rows, query_back)
        + dot_rows(grad_key_rows, key_back)
        + dot_rows(grad_value_rows, value_back)
    )
    grad_query = dot_cols(normed_one, grad_query_rows)
    grad_key = dot_cols(normed_one, grad_key_rows)
    grad_value = dot_cols(normed_one, grad_value_rows)
    grad_norm_one, grad_gain_attn = norm_back(grad_normed_one, unit_one, factor_one, gain_one)
    grad_input = (grad_hidden + grad_norm_one).astype(jnp.bfloat16)
    attn_owned = tuple(
        (
            part.astype(jnp.float32)
            for part in sent_together(
                (
                    grad_gain_attn.astype(jnp.bfloat16),
                    grad_query.astype(jnp.bfloat16),
                    grad_key.astype(jnp.bfloat16),
                    grad_value.astype(jnp.bfloat16),
                    grad_out.astype(jnp.bfloat16),
                ),
                "fsdp",
                0,
                1,
            )
        )
    )
    summed = (
        lax.psum(attn_owned[0].astype(jnp.bfloat16), "rep").astype(jnp.float32),
        lax.psum(attn_owned[1].astype(jnp.bfloat16), "rep").astype(jnp.float32),
        lax.psum(attn_owned[2].astype(jnp.bfloat16), "rep").astype(jnp.float32),
        lax.psum(attn_owned[3].astype(jnp.bfloat16), "rep").astype(jnp.float32),
        lax.psum(attn_owned[4].astype(jnp.bfloat16), "rep").astype(jnp.float32),
        lax.psum(ffn_owned[0].astype(jnp.bfloat16), "rep").astype(jnp.float32),
        lax.psum(ffn_owned[1].astype(jnp.bfloat16), "rep").astype(jnp.float32),
        lax.psum(ffn_owned[2].astype(jnp.bfloat16), "rep").astype(jnp.float32),
        lax.psum(ffn_owned[4].astype(jnp.bfloat16), "rep").astype(jnp.float32),
        lax.psum(ffn_owned[3].astype(jnp.bfloat16), "rep").astype(jnp.float32),
        lax.psum(ffn_owned[5].astype(jnp.bfloat16), "rep").astype(jnp.float32),
    )
    return (
        result.astype(jnp.bfloat16),
        grad_input,
        summed[0],
        summed[1],
        summed[2],
        summed[3],
        summed[4],
        summed[5],
        summed[6],
        summed[7],
        summed[8],
        summed[9],
        summed[10],
    )


def solution(mesh):
    return jax.shard_map(
        shards,
        mesh=mesh,
        in_specs=(
            P(("rep", "fsdp"), None),
            P("rep"),
            P(("rep", "fsdp"), None),
            P("fsdp"),
            P("fsdp", None),
            P("fsdp", None),
            P("fsdp", None),
            P("fsdp", None),
            P("fsdp"),
            P("fsdp", None),
            P("fsdp", None),
            P("fsdp", None),
            P("fsdp", None, None),
            P(None, "fsdp", None),
            P(("rep", "fsdp"), None),
        ),
        out_specs=(
            P(("rep", "fsdp"), None),
            P(("rep", "fsdp"), None),
            P("fsdp"),
            P("fsdp", None),
            P("fsdp", None),
            P("fsdp", None),
            P("fsdp", None),
            P("fsdp"),
            P("fsdp", None),
            P("fsdp", None),
            P("fsdp", None),
            P("fsdp", None, None),
            P(None, "fsdp", None),
        ),
        check_vma=False,
    )
```

profile of v0, /device:TPU:1, one launch (start us, length us, event | category | flops | bytes accessed | tf_op | source)
XLA Modules:
  0.0 1894.8 jit_solution(13531483751671472540)
XLA Ops:
  10.9 116.5 %all-gather.11.cloned.1.call-done = bf16[1536,2561]{1,0:T(8,128)(2,1)} async-done(((bf16[192,2561]{1,0:T(8,128)(2,1)}), bf16[1536,2561]{1,0:T(8,128)(2,1)}) %all-gather.11.cloned.1.call-update) | async-done | bytes 7867408 | tf_op jit(solution)/shard_map/all_gather | solution.py:20
  148.5 16.4 all-reduce
  164.9 27.8 %all-gather.1 = bf16[8,192,8]{1,2,0:T(8,128)(2,1)S(1)} all-gather(bf16[1,192,8]{1,2,0:T(8,128)(2,1)S(1)} %bitcast.143), channel_id=1, replica_groups=mesh['rep'=32,'fsdp'=8] {'fsdp'}, dimensions={0}, use_global_device_ids=true | all-gather | bytes 27648 | tf_op jit(solution)/shard_map/all_gather | solution.py:174
  210.6 64.4 %all-gather.15.cloned.1.call-done = bf16[1536,1536]{1,0:T(8,128)(2,1)} async-done(((bf16[192,1536]{1,0:T(8,128)(2,1)}), bf16[1536,1536]{1,0:T(8,128)(2,1)}) %all-gather.15.cloned.1.call-update) | async-done | bytes 4718608 | tf_op jit(solution)/shard_map/all_gather | solution.py:170
  281.7 88.5 %all-gather.19.cloned.1.call-done = bf16[1536,2048]{1,0:T(8,128)(2,1)} async-done(((bf16[192,2048]{1,0:T(8,128)(2,1)}), bf16[1536,2048]{1,0:T(8,128)(2,1)}) %all-gather.19.cloned.1.call-update) | async-done | bytes 6291472 | tf_op jit(solution)/shard_map/all_gather | solution.py:175
  375.0 177.1 %all-gather.25.cloned.1.call-done = bf16[7864320]{0:T(1024)(128)(2,1)} async-done(((bf16[983040]{0:T(1024)(128)(2,1)}), bf16[7864320]{0:T(1024)(128)(2,1)}) %all-gather.25.cloned.1.call-update) | async-done | bytes 15728656 | tf_op jit(solution)/shard_map/all_gather | solution.py:44
  552.1 20.6 %reshape.239 = bf16[8,983040]{1,0:T(8,128)(2,1)} reshape(bf16[7864320]{0:T(1024)(128)(2,1)} %all-gather.25.cloned.1.call-done) | data formatting | bytes 31457280 | tf_op jit(solution)/shard_map/all_gather | solution.py:44
  572.6 10.8 slice.46
  586.6 13.2 copy.156
  602.0 219.1 %all-gather.17.cloned.1.call-done = bf16[1536,8,1024]{2,0,1:T(8,128)(2,1)} async-done(((bf16[192,8,1024]{2,0,1:T(8,128)(2,1)}), bf16[1536,8,1024]{2,0,1:T(8,128)(2,1)}) %all-gather.17.cloned.1.call-update) | async-done | bytes 25165840 | tf_op jit(solution)/shard_map/all_gather | solution.py:176
  821.1 10.0 fusion.78
  831.1 10.4 fusion.35
  853.2 13.4 convolution_bitcast_fusion.1
  913.4 56.0 %reduce-scatter.7.cloned.1.call-done = bf16[128,1024]{1,0:T(8,128)(2,1)} async-done(((bf16[1024,1024]{1,0:T(8,128)(2,1)}), bf16[128,1024]{1,0:T(8,128)(2,1)}) %reduce-scatter.7.cloned.1.call-update) | async-done | bytes 262160
  977.6 63.8 %concatenate.35 = bf16[1536,4097]{0,1:T(8,128)(2,1)} concatenate(bf16[1536,1]{0,1:T(2,128)(2,1)S(1)} %convert_element_type.236, bf16[1536,1536]{0,1:T(8,128)(2,1)} %convolution_convert_fusion, bf16[1536,512]{0,1:T(8,128)(2,1)S(1)} %convolution_convert_fusion.3, bf16[1536,512]{0,1:T(8,128)(2,1)} %convolution_convert_fusion.2, bf16[1536,1536]{0,1:T(8,128)(2,1)} %convolution_convert_fusion.1), dimensions={1} | concatenate | bytes 25171968 | tf_op jit(solution)/shard_map/concatenate | solution.py:72
  1041.4 16.6 copy.206
  1058.7 75.8 %all-gather.23.cloned.1.call-done = bf16[1024,6656]{1,0:T(8,128)(2,1)} async-done(((bf16[128,6656]{1,0:T(8,128)(2,1)}), bf16[1024,6656]{1,0:T(8,128)(2,1)}) %all-gather.23.cloned.1.call-update) | async-done | bytes 13631504 | tf_op jit(solution)/shard_map/all_gather | solution.py:20
  1142.3 11.9 copy.203
  1164.2 133.3 %reduce-scatter.9.cloned.1.call-done = bf16[192,4097]{1,0:T(8,128)(2,1)} async-done(((bf16[1536,4097]{1,0:T(8,128)(2,1)}), bf16[192,4097]{1,0:T(8,128)(2,1)}) %reduce-scatter.9.cloned.1.call-update) | async-done | bytes 1573264
  1304.5 279.1 %all-gather.21.cloned.1.call-done = bf16[1024,11784]{0,1:T(8,128)(2,1)} async-done(((bf16[128,11784]{0,1:T(8,128)(2,1)}), bf16[1024,11784]{0,1:T(8,128)(2,1)}) %all-gather.21.cloned.1.call-update) | async-done | bytes 24133648 | tf_op jit(solution)/shard_map/all_gather | solution.py:20
  1587.5 13.8 split.73
  1601.3 13.2 convolution_convert_fusion.5
  1635.2 56.7 %all-reduce.1 = (bf16[192]{0:T(256)(128)(2,1)S(1)}, bf16[192]{0:T(256)(128)(2,1)S(1)}, bf16[192,8]{0,1:T(8,128)(2,1)S(1)}) all-reduce(bf16[192]{0:T(256)(128)(2,1)S(1)} %slice_reduce_fusion, bf16[192]{0:T(256)(128)(2,1)S(1)} %reduce_sum.129, bf16[192,8]{0,1:T(8,128)(2,1)S(1)} %convolution_convert_fusion.6), channel_id=1, replica_groups=mesh['rep'=32,'fsdp'=8] {'rep'}, use_global_device_ids=true, to_apply=%region_14.15 | all-reduce | flops 1920 | bytes 7680 | tf_op jit(solution)/shard_map/psum | solution.py:332
  1693.6 177.9 %all-reduce.5.cloned.1.call-done = (bf16[192,1536]{0,1:T(8,128)(2,1)}, bf16[192,512]{0,1:T(8,128)(2,1)}, bf16[192,512]{0,1:T(8,128)(2,1)}, bf16[192,1536]{0,1:T(...) async-done(((bf16[192,1536]{0,1:T(8,128)(2,1)}, bf16[192,512]{0,1:T(8,128)(2,1)}, ...) | async-done | bytes 7471120 | tf_op jit(solution)/shard_map/psum | solution.py:333
  (260 shorter events, 192.9 us)
Async XLA Ops:
  7.2 120.2 %all-gather.11.cloned.1.call-start = ((), (), s32[]{:S(2)}) async-start(), calls=%async_computation.3 | async-start | bytes 9289728 | tf_op jit(solution)/shard_map/all_gather | solution.py:20
  10.7 187.1 %all-gather.13.cloned.1.call-start = ((), (), s32[]{:S(2)}) async-start(), calls=%async_computation.4 | async-start | bytes 2359296 | tf_op jit(solution)/shard_map/all_gather | solution.py:33
  10.9 182.5 %copy-start.48 = (f32[128]{0:T(128)}, f32[128]{0:T(128)S(1)}, u32[]{:S(2)}) copy-start(f32[128]{0:T(128)S(1)} %add_rsqrt_fusion.1) | copy-start | bytes 1540
  134.1 140.9 %all-gather.15.cloned.1.call-start = ((), (), s32[]{:S(2)}) async-start(), calls=%async_computation.5 | async-start | bytes 5308416 | tf_op jit(solution)/shard_map/all_gather | solution.py:170
  134.9 235.3 %all-gather.19.cloned.1.call-start = ((), (), s32[]{:S(2)}) async-start(), calls=%async_computation.7 | async-start | bytes 7077888 | tf_op jit(solution)/shard_map/all_gather | solution.py:175
  135.4 416.6 %all-gather.25.cloned.1.call-start = ((), (), s32[]{:S(2)}) async-start(), calls=%async_computation.10 | async-start | bytes 17694720 | tf_op jit(solution)/shard_map/all_gather | solution.py:44
  141.0 680.1 %all-gather.17.cloned.1.call-start = ((), (), s32[]{:S(2)}) async-start(), calls=%async_computation.6 | async-start | bytes 28311552 | tf_op jit(solution)/shard_map/all_gather | solution.py:176
  146.3 18.6 copy-start.52
  146.3 46.6 %copy-start.45 = (s32[1024]{0:T(1024)S(1)}, s32[1024]{0:T(1024)}, u32[]{:S(2)}) copy-start(s32[1024]{0:T(1024)} %param.16) | copy-start | bytes 12292
  146.3 46.6 %copy-start.53 = (s32[128,6]{0,1:T(8,128)S(1)}, s32[128,6]{0,1:T(8,128)}, u32[]{:S(2)}) copy-start(s32[128,6]{0,1:T(8,128)} %param.17) | copy-start | bytes 9220
  146.4 823.0 %reduce-scatter.7.cloned.1.call-start = ((), (), s32[]{:S(2)}) async-start(), calls=%async_computation.11 | async-start | bytes 2359296
  164.9 113.4 %copy-start.40 = (f32[1536]{0:T(1024)}, f32[1536]{0:T(1024)S(1)}, u32[]{:S(2)}) copy-start(f32[1536]{0:T(1024)S(1)} %convert_element_type.213) | copy-start | bytes 18436
  192.9 86.7 %copy-start.38 = (bf16[1536,8]{0,1:T(8,128)(2,1)}, bf16[1536,8]{0,1:T(8,128)(2,1)S(1)}, u32[]{:S(2)}) copy-start(bf16[1536,8]{0,1:T(8,128)(2,1)S(1)} %reshape.244) | copy-start | bytes 73732
  210.6 67.7 %copy-start.23 = (bf16[4,128,3,128]{3,1,2,0:T(8,128)(2,1)}, bf16[4,128,3,128]{3,1,2,0:T(8,128)(2,1)S(1)}, u32[]{:S(2)}) copy-start(bf16[4,128,3,128]{3,1,2,0:T(8,128)(2,1)S(1)} %fusion.45) | copy-start | bytes 1179652
  278.3 96.7 %copy-start.50 = (f32[128]{0:T(128)}, f32[128]{0:T(128)S(1)}, u32[]{:S(2)}) copy-start(f32[128]{0:T(128)S(1)} %add_rsqrt_fusion) | copy-start | bytes 1540
  279.3 95.7 %copy-start.8 = (bf16[128,1536]{1,0:T(8,128)(2,1)}, bf16[128,1536]{1,0:T(8,128)(2,1)S(1)}, u32[]{:S(2)}) copy-start(bf16[128,1536]{1,0:T(8,128)(2,1)S(1)} %multiply_convert_fusion.1) | copy-start | bytes 1179652
  586.6 13.2 copy-start.29
  599.7 221.3 %copy-start.9 = (bf16[128,1536]{1,0:T(8,128)(2,1)S(1)}, bf16[128,1536]{1,0:T(8,128)(2,1)}, u32[]{:S(2)}) copy-start(bf16[128,1536]{1,0:T(8,128)(2,1)} %copy-done.8) | copy-start | bytes 1179652
  601.7 229.4 %copy-start.30 = (bf16[128,1024]{1,0:T(8,128)(2,1)}, bf16[128,1024]{1,0:T(8,128)(2,1)S(1)}, u32[]{:S(2)}) copy-start(bf16[128,1024]{1,0:T(8,128)(2,1)S(1)} %get-tuple-element.106) | copy-start | bytes 786436
  891.8 242.6 %all-gather.23.cloned.1.call-start = ((), (), s32[]{:S(2)}) async-start(), calls=%async_computation.9 | async-start | bytes 15335424 | tf_op jit(solution)/shard_map/all_gather | solution.py:20
  901.6 395.9 %reduce-scatter.9.cloned.1.call-start = ((), (), s32[]{:S(2)}) async-start(), calls=%async_computation.12 | async-start | bytes 14598144
  1058.0 525.6 %all-gather.21.cloned.1.call-start = ((), (), s32[]{:S(2)}) async-start(), calls=%async_computation.8 | async-start | bytes 27150336 | tf_op jit(solution)/shard_map/all_gather | solution.py:20
  1058.6 812.9 %all-reduce.5.cloned.1.call-start = ((), (), s32[]{:S(2)}) async-start(), calls=%async_computation.13 | async-start | bytes 15990784 | tf_op jit(solution)/shard_map/psum | solution.py:333
  1620.6 11.4 all-to-all-start
  (51 other events, 270.4 us)
Sparse Core Ops, SparseCore 0:
  11.2 116.1 all-gather.10
  134.2 57.2 all-gather.12
  194.2 80.7 all-gather.14
  277.5 92.6 all-gather.18
  372.7 179.3 all-gather.24
  555.0 265.9 all-gather.16
  891.9 77.3 reduce-scatter.6
  972.3 162.0 all-gather.22
  1139.3 158.1 reduce-scatter.8
  1299.8 283.7 all-gather.20
  1619.4 252.0 all-reduce.4
where the time goes:
time: 1910 us; the launch traced here: 1890 us
  waiting for transfers between devices  1390 us (73%)
  local copies, waits for them, and re-layouts  232 us (12%)
  matrix products  130 us (7%)
  blocking collectives  101 us (5%)
  other arithmetic  23.6 us (1%)
    all_gather x3, waiting for transfers between devices, side_by_side(): whole = lax.all_gather(both, axis, axis=dim, tiled=True)  471 us
    all_gather x1, waiting for transfers between devices, shards(): lax.all_gather(w_expert_in, 'fsdp', axis=0, tiled=True)  219 us
    unnamed x13, waiting for transfers between devices  191 us
    psum x1, waiting for transfers between devices, shards(): lax.psum(attn_owned[1].astype(jnp.bfloat16), 'rep').astype(jnp.float32)  178 us
    all_gather x1, waiting for transfers between devices, gather_packed(): lines, at, gathered = (lax.all_gather(flat, axis), 0, [])  177 us
    all_gather x1, waiting for transfers between devices, shards(): lax.all_gather(w_shared_in, 'fsdp', axis=0, tiled=True)  88.5 us
    all_gather x1, waiting for transfers between devices, shards(): out_full = lax.all_gather(w_out, 'fsdp', axis=0, tiled=True)  64.4 us
    concatenate x1, local copies, waits for them, and re-layouts, sent_together(): both = jnp.concatenate(columns, axis=along)  63.8 us
  transfers between devices with their start and end apart: 12, of which 10 were waited for; matrix products, arithmetic and copies ran while one was open for 13% of the time, Pallas kernels for 0%

commit v1 on v0

--- a/solution.py
+++ b/solution.py
@@ -167,7 +167,10 @@
     probs = (expo / total).astype(jnp.bfloat16)
     attended = jnp.einsum("kgts,skd->tkgd", probs, value_heads, preferred_element_type=jnp.float32)
     attended = attended.reshape(local_rows, HEADS * HEAD).astype(jnp.bfloat16)
-    out_full = lax.all_gather(w_out, "fsdp", axis=0, tiled=True)
+    parts_out = jax.lax.axis_size("fsdp")
+    raw_out = jnp.stack([w_out] * parts_out)
+    t_next = jax.lax.all_to_all(raw_out, concat_axis=0, split_axis=0, axis_name="fsdp")
+    out_full = jnp.concatenate(t_next, axis=0)
     hidden = inputs + jnp.dot(attended, out_full, preferred_element_type=jnp.float32)
     ffn_in = (
         lax.all_gather(gain_ffn, "fsdp", axis=0, tiled=True),

time: 1910 us -> 1870 us (0.979)
  waiting for transfers between devices: 1390 us -> 1280 us
  blocking collectives: 101 us -> 163 us
    all_gather x1 -> x0, waiting for transfers between devices: 64.4 us -> none  [shards(): out_full = lax.all_gather(w_out, 'fsdp', axis=0, tiled=True)]
    unnamed x1, blocking collectives: 16.4 us -> 78.5 us
    all_gather x1, waiting for transfers between devices: 88.5 us -> 42.7 us  [shards(): lax.all_gather(w_shared_in, 'fsdp', axis=0, tiled=True)]
    unnamed x142 -> x144, local copies, waits for them, and re-layouts: 51.8 us -> 52.3 us
    unnamed x13 -> x12, waiting for transfers between devices: 191 us -> 191 us
  transfers between devices with their start and end apart: 12 -> 12, of which waited for: 10 -> 9; matrix products, arithmetic and copies ran while one was open for 13% -> 13% of each run, Pallas kernels for 0% -> 0%
where the time goes in v1:
time: 1870 us; the launch traced here: 1850 us
  waiting for transfers between devices  1280 us (68%)
  local copies, waits for them, and re-layouts  235 us (13%)
  blocking collectives  163 us (9%)
  matrix products  130 us (7%)
  other arithmetic  23.5 us (1%)
    all_gather x3, waiting for transfers between devices, side_by_side(): whole = lax.all_gather(both, axis, axis=dim, tiled=True)  471 us
    all_gather x1, waiting for transfers between devices, shards(): lax.all_gather(w_expert_in, 'fsdp', axis=0, tiled=True)  219 us
    unnamed x12, waiting for transfers between devices  191 us
    psum x1, waiting for transfers between devices, shards(): lax.psum(attn_owned[1].astype(jnp.bfloat16), 'rep').astype(jnp.float32)  178 us
    all_gather x1, waiting for transfers between devices, gather_packed(): lines, at, gathered = (lax.all_gather(flat, axis), 0, [])  177 us
    unnamed x1, blocking collectives  78.5 us
    concatenate x1, local copies, waits for them, and re-layouts, sent_together(): both = jnp.concatenate(columns, axis=along)  63.7 us
    psum x1, blocking collectives, shards(): lax.psum(attn_owned[0].astype(jnp.bfloat16), 'rep').astype(jnp.float32)  56.9 us
  transfers between devices with their start and end apart: 12, of which 9 were waited for; matrix products, arithmetic and copies ran while one was open for 13% of the time, Pallas kernels for 0%

profile of v1, /device:TPU:1, one launch (start us, length us, event | category | flops | bytes accessed | tf_op | source)
XLA Modules:
  0.0 1854.5 jit_solution(3741494863714712255)
XLA Ops:
  10.9 116.5 %all-gather.10.cloned.1.call-done = bf16[1536,2561]{1,0:T(8,128)(2,1)} async-done(((bf16[192,2561]{1,0:T(8,128)(2,1)}), bf16[1536,2561]{1,0:T(8,128)(2,1)}) %all-gather.10.cloned.1.call-update) | async-done | bytes 7867408 | tf_op jit(solution)/shard_map/all_gather | solution.py:20
  155.8 78.5 %all-reduce = bf16[1536]{0:T(1024)(128)(2,1)S(1)} all-reduce(bf16[1536]{0:T(1024)(128)(2,1)S(1)} %dynamic-update-slice), channel_id=1, replica_groups=mesh['rep'=32,'fsdp'=8] {'fsdp'}, use_global_device_ids=true, to_apply=%add | all-reduce | flops 1536 | bytes 6144
  234.3 27.7 %all-gather.1 = bf16[8,192,8]{1,2,0:T(8,128)(2,1)S(1)} all-gather(bf16[1,192,8]{1,2,0:T(8,128)(2,1)S(1)} %bitcast.144), channel_id=1, replica_groups=mesh['rep'=32,'fsdp'=8] {'fsdp'}, dimensions={0}, use_global_device_ids=true | all-gather | bytes 27648 | tf_op jit(solution)/shard_map/all_gather | solution.py:177
  286.7 42.7 %all-gather.16.cloned.1.call-done = bf16[1536,2048]{1,0:T(8,128)(2,1)} async-done(((bf16[192,2048]{1,0:T(8,128)(2,1)}), bf16[1536,2048]{1,0:T(8,128)(2,1)}) %all-gather.16.cloned.1.call-update) | async-done | bytes 6291472 | tf_op jit(solution)/shard_map/all_gather | solution.py:178
  334.1 177.1 %all-gather.22.cloned.1.call-done = bf16[7864320]{0:T(1024)(128)(2,1)} async-done(((bf16[983040]{0:T(1024)(128)(2,1)}), bf16[7864320]{0:T(1024)(128)(2,1)}) %all-gather.22.cloned.1.call-update) | async-done | bytes 15728656 | tf_op jit(solution)/shard_map/all_gather | solution.py:44
  511.2 20.6 %reshape.246 = bf16[8,983040]{1,0:T(8,128)(2,1)} reshape(bf16[7864320]{0:T(1024)(128)(2,1)} %all-gather.22.cloned.1.call-done) | data formatting | bytes 31457280 | tf_op jit(solution)/shard_map/all_gather | solution.py:44
  531.8 10.8 slice.46
  545.7 13.2 copy.156
  561.2 219.1 %all-gather.14.cloned.1.call-done = bf16[1536,8,1024]{2,0,1:T(8,128)(2,1)} async-done(((bf16[192,8,1024]{2,0,1:T(8,128)(2,1)}), bf16[1536,8,1024]{2,0,1:T(8,128)(2,1)}) %all-gather.14.cloned.1.call-update) | async-done | bytes 25165840 | tf_op jit(solution)/shard_map/all_gather | solution.py:179
  780.2 10.0 fusion.78
  790.3 10.4 fusion.35
  812.4 13.4 convolution_bitcast_fusion.1
  872.6 56.0 %reduce-scatter.7.cloned.1.call-done = bf16[128,1024]{1,0:T(8,128)(2,1)} async-done(((bf16[1024,1024]{1,0:T(8,128)(2,1)}), bf16[128,1024]{1,0:T(8,128)(2,1)}) %reduce-scatter.7.cloned.1.call-update) | async-done | bytes 262160
  936.8 63.7 %concatenate.35 = bf16[1536,4097]{0,1:T(8,128)(2,1)} concatenate(bf16[1536,1]{0,1:T(2,128)(2,1)S(1)} %convert_element_type.238, bf16[1536,1536]{0,1:T(8,128)(2,1)} %convolution_convert_fusion, bf16[1536,512]{0,1:T(8,128)(2,1)S(1)} %convolution_convert_fusion.3, bf16[1536,512]{0,1:T(8,128)(2,1)} %convolution_convert_fusion.2, bf16[1536,1536]{0,1:T(8,128)(2,1)} %convolution_convert_fusion.1), dimensions={1} | concatenate | bytes 25171968 | tf_op jit(solution)/shard_map/concatenate | solution.py:72
  1000.6 16.6 copy.206
  1018.0 75.6 %all-gather.20.cloned.1.call-done = bf16[1024,6656]{1,0:T(8,128)(2,1)} async-done(((bf16[128,6656]{1,0:T(8,128)(2,1)}), bf16[1024,6656]{1,0:T(8,128)(2,1)}) %all-gather.20.cloned.1.call-update) | async-done | bytes 13631504 | tf_op jit(solution)/shard_map/all_gather | solution.py:20
  1093.5 7.9 split.74
  1101.4 11.9 copy.203
  1123.3 133.3 %reduce-scatter.9.cloned.1.call-done = bf16[192,4097]{1,0:T(8,128)(2,1)} async-done(((bf16[1536,4097]{1,0:T(8,128)(2,1)}), bf16[192,4097]{1,0:T(8,128)(2,1)}) %reduce-scatter.9.cloned.1.call-update) | async-done | bytes 1573264
  1263.6 279.2 %all-gather.18.cloned.1.call-done = bf16[1024,11784]{0,1:T(8,128)(2,1)} async-done(((bf16[128,11784]{0,1:T(8,128)(2,1)}), bf16[1024,11784]{0,1:T(8,128)(2,1)}) %all-gather.18.cloned.1.call-update) | async-done | bytes 24133648 | tf_op jit(solution)/shard_map/all_gather | solution.py:20
  1546.7 13.8 split.73
  1560.6 13.2 convolution_convert_fusion.5
  1594.5 56.9 %all-reduce.1 = (bf16[192]{0:T(256)(128)(2,1)S(1)}, bf16[192]{0:T(256)(128)(2,1)S(1)}, bf16[192,8]{0,1:T(8,128)(2,1)S(1)}) all-reduce(bf16[192]{0:T(256)(128)(2,1)S(1)} %slice_reduce_fusion, bf16[192]{0:T(256)(128)(2,1)S(1)} %reduce_sum.129, bf16[192,8]{0,1:T(8,128)(2,1)S(1)} %convolution_convert_fusion.6), channel_id=1, replica_groups=mesh['rep'=32,'fsdp'=8] {'rep'}, use_global_device_ids=true, to_apply=%region_14.15 | all-reduce | flops 1920 | bytes 7680 | tf_op jit(solution)/shard_map/psum | solution.py:335
  1653.1 177.9 %all-reduce.5.cloned.1.call-done = (bf16[192,1536]{0,1:T(8,128)(2,1)}, bf16[192,512]{0,1:T(8,128)(2,1)}, bf16[192,512]{0,1:T(8,128)(2,1)}, bf16[192,1536]{0,1:T(...) async-done(((bf16[192,1536]{0,1:T(8,128)(2,1)}, bf16[192,512]{0,1:T(8,128)(2,1)}, ...) | async-done | bytes 7471120 | tf_op jit(solution)/shard_map/psum | solution.py:336
  (262 shorter events, 192.6 us)
Async XLA Ops:
  7.2 120.2 %all-gather.10.cloned.1.call-start = ((), (), s32[]{:S(2)}) async-start(), calls=%async_computation.4 | async-start | bytes 9289728 | tf_op jit(solution)/shard_map/all_gather | solution.py:20
  10.7 256.4 %all-gather.12.cloned.1.call-start = ((), (), s32[]{:S(2)}) async-start(), calls=%async_computation.5 | async-start | bytes 2359296 | tf_op jit(solution)/shard_map/all_gather | solution.py:33
  10.9 251.7 %copy-start.49 = (f32[128]{0:T(128)}, f32[128]{0:T(128)S(1)}, u32[]{:S(2)}) copy-start(f32[128]{0:T(128)S(1)} %add_rsqrt_fusion.1) | copy-start | bytes 1540
  134.1 195.2 %all-gather.16.cloned.1.call-start = ((), (), s32[]{:S(2)}) async-start(), calls=%async_computation.7 | async-start | bytes 7077888 | tf_op jit(solution)/shard_map/all_gather | solution.py:178
  134.9 376.4 %all-gather.22.cloned.1.call-start = ((), (), s32[]{:S(2)}) async-start(), calls=%async_computation.10 | async-start | bytes 17694720 | tf_op jit(solution)/shard_map/all_gather | solution.py:44
  140.4 639.8 %all-gather.14.cloned.1.call-start = ((), (), s32[]{:S(2)}) async-start(), calls=%async_computation.6 | async-start | bytes 28311552 | tf_op jit(solution)/shard_map/all_gather | solution.py:179
  149.4 84.9 %copy-start.53 = (bf16[192,8]{0,1:T(8,128)(2,1)S(1)}, bf16[192,8]{0,1:T(8,128)(2,1)}, u32[]{:S(2)}) copy-start(bf16[192,8]{0,1:T(8,128)(2,1)} %param.24) | copy-start | bytes 9220
  149.4 112.7 %copy-start.46 = (s32[1024]{0:T(1024)S(1)}, s32[1024]{0:T(1024)}, u32[]{:S(2)}) copy-start(s32[1024]{0:T(1024)} %param.16) | copy-start | bytes 12292
  149.4 112.8 %copy-start.54 = (s32[128,6]{0,1:T(8,128)S(1)}, s32[128,6]{0,1:T(8,128)}, u32[]{:S(2)}) copy-start(s32[128,6]{0,1:T(8,128)} %param.17) | copy-start | bytes 9220
  149.4 130.5 %all-to-all-start = ((bf16[8,192,1536]{2,1,0:T(8,128)(2,1)}), bf16[8,192,1536]{2,1,0:T(8,128)(2,1)}, u32[]{:S(2)}, u32[]{:S(2)}) async-start(bf16[8,192,1536]{2,1,0:T(8,128)(2,1)} %stack.2), calls=%async_computation | async-start | bytes 9437184 | tf_op jit(solution)/shard_map/all_to_all | solution.py:172
  154.2 774.4 %reduce-scatter.7.cloned.1.call-start = ((), (), s32[]{:S(2)}) async-start(), calls=%async_computation.11 | async-start | bytes 2359296
  234.3 49.0 %copy-start.41 = (f32[1536]{0:T(1024)}, f32[1536]{0:T(1024)S(1)}, u32[]{:S(2)}) copy-start(f32[1536]{0:T(1024)S(1)} %convert_element_type.215) | copy-start | bytes 18436
  262.1 22.4 %copy-start.39 = (bf16[1536,8]{0,1:T(8,128)(2,1)}, bf16[1536,8]{0,1:T(8,128)(2,1)S(1)}, u32[]{:S(2)}) copy-start(bf16[1536,8]{0,1:T(8,128)(2,1)S(1)} %reshape.251) | copy-start | bytes 73732
  283.3 50.8 %copy-start.51 = (f32[128]{0:T(128)}, f32[128]{0:T(128)S(1)}, u32[]{:S(2)}) copy-start(f32[128]{0:T(128)S(1)} %add_rsqrt_fusion) | copy-start | bytes 1540
  284.3 49.8 %copy-start.8 = (bf16[128,1536]{1,0:T(8,128)(2,1)}, bf16[128,1536]{1,0:T(8,128)(2,1)S(1)}, u32[]{:S(2)}) copy-start(bf16[128,1536]{1,0:T(8,128)(2,1)S(1)} %multiply_convert_fusion.1) | copy-start | bytes 1179652
  545.7 13.2 copy-start.27
  545.7 13.2 copy-start.29
  558.9 221.3 %copy-start.9 = (bf16[128,1536]{1,0:T(8,128)(2,1)S(1)}, bf16[128,1536]{1,0:T(8,128)(2,1)}, u32[]{:S(2)}) copy-start(bf16[128,1536]{1,0:T(8,128)(2,1)} %copy-done.8) | copy-start | bytes 1179652
  560.8 229.4 %copy-start.30 = (bf16[128,1024]{1,0:T(8,128)(2,1)}, bf16[128,1024]{1,0:T(8,128)(2,1)S(1)}, u32[]{:S(2)}) copy-start(bf16[128,1024]{1,0:T(8,128)(2,1)S(1)} %get-tuple-element.106) | copy-start | bytes 786436
  851.0 242.6 %all-gather.20.cloned.1.call-start = ((), (), s32[]{:S(2)}) async-start(), calls=%async_computation.9 | async-start | bytes 15335424 | tf_op jit(solution)/shard_map/all_gather | solution.py:20
  860.8 395.9 %reduce-scatter.9.cloned.1.call-start = ((), (), s32[]{:S(2)}) async-start(), calls=%async_computation.12 | async-start | bytes 14598144
  1017.2 525.7 %all-gather.18.cloned.1.call-start = ((), (), s32[]{:S(2)}) async-start(), calls=%async_computation.8 | async-start | bytes 27150336 | tf_op jit(solution)/shard_map/all_gather | solution.py:20
  1017.9 813.0 %all-reduce.5.cloned.1.call-start = ((), (), s32[]{:S(2)}) async-start(), calls=%async_computation.13 | async-start | bytes 15990784 | tf_op jit(solution)/shard_map/psum | solution.py:336
  1579.9 11.4 all-to-all-start.1
  (52 other events, 271.2 us)
Sparse Core Ops, SparseCore 0:
  11.2 116.1 all-gather.9
  134.3 98.3 all-gather.11
  235.3 94.0 all-gather.15
  331.8 179.3 all-gather.21
  514.2 265.9 all-gather.13
  851.1 77.3 reduce-scatter.6
  931.5 161.9 all-gather.19
  1098.4 158.2 reduce-scatter.8
  1259.1 283.7 all-gather.17
  1578.7 252.2 all-reduce.4
